TPU v7x, 128 devices: a whole 4x4x4 slice. The times are simulated.
128 devices in a mesh: row: 8 (over z, core), col: 16 (over x, y).
Axes of the slice: x: 4, y: 4, z: 4, core: 2. Of those that a mesh axis runs over, the one named last changes fastest.
Arguments:
- start_block: float32 [32768, 128], P(('row', 'col')), may hold values from -6 to 6
- degree: float32 [32768], P(('row', 'col')), may hold values from 3.99 to 4.01
- block_values: float32 [49152, 4096], P(('row', 'col')), may hold values from -0.0007324219 to 0.0007324219
- block_rows: int32 [49152], P(('row', 'col')), may hold values from 0 to 31
- block_slots: int32 [49152], P(('row', 'col')), may hold values from 0 to 31, as said below
- need_lists: int32 [2048, 2], P(('row', 'col')), may hold values from 0 to 4, as said below
- live_blocks: int32 [128], P(('row', 'col')), may hold values from 96 to 384, as said below
Outputs:
- alphas: float32 [2, 128, 128], replicated
- betas: float32 [2, 128, 128], replicated
- next_basis: float32 [32768, 128], P(('row', 'col'))
Inputs may be any that keep to these rules, and one draw needn't show every extreme that they name: `need_lists`: entries of a need list are distinct block rows, listed first, then padded with 4; every list has at least one entry, and on every device some list is full with 2 entries. `block_slots`: each slot's value p * 2 + q points at a listed (never padded) entry q of the device's need list p. `live_blocks`: some device uses all 384 slots in every draw.
All inputs are finite; a program needn't handle non-finite values.
Results may differ from a plain program's by a relative error of at most 0.00045.
Values sent between devices are 32-bit elements; how exact they have to be, the bound alone decides.
No kernel may reach another device: no remote copies, remote signals or barrier semaphores. Data moves between devices by JAX's collectives and lax.ppermute only.
A program may use at most 128 MiB of HBM per device.

v0:
```python
import jax
import jax.numpy as jnp
from jax import lax
from jax.sharding import PartitionSpec as P

BS = 64
ITERS = 2
HIGH = lax.Precision.HIGHEST


def local_gram(left, right):
    return jnp.einsum("ra,rb->ab", left, right, precision=HIGH)


def on_device(start_block, degree, block_values, block_rows, block_slots, need_lists, live_blocks):
    row_count = lax.axis_size("row")
    col_count = lax.axis_size("col")
    local_rows, block_width = start_block.shape
    owned_blocks = local_rows // BS
    list_length = need_lists.shape[1]
    capacity = block_values.shape[0]
    group_size = min(128, capacity)
    total_rows = local_rows * row_count * col_count
    live_count = live_blocks[0]
    flat_need = need_lists.reshape(-1)
    stripe_cols = block_slots // list_length * owned_blocks + flat_need[block_slots]
    start_gram = lax.psum(local_gram(start_block, start_block), ("row", "col")) / total_rows
    lower_factor = jnp.linalg.cholesky(start_gram)
    current = lax.linalg.triangular_solve(
        lower_factor, start_block, left_side=False, lower=True, transpose_a=True
    )
    basis_list = [current]
    alpha_list = []
    beta_list = []
    for iteration in range(ITERS):
        owned_rows = current.reshape(owned_blocks, BS, block_width)
        row_side = lax.all_gather(owned_rows, "row", axis=0, tiled=True)
        col_side = lax.all_gather(owned_rows, "col", axis=0, tiled=True)
        col_length = col_count * owned_blocks
        group_total = (live_count + group_size - 1) // group_size

        def group_step(group_index, partials):
            row_part, col_part = partials
            first_slot = group_index * group_size
            values_now = lax.dynamic_slice_in_dim(block_values, first_slot, group_size, 0).reshape(
                group_size, BS, BS
            )
            rows_now = lax.dynamic_slice_in_dim(block_rows, first_slot, group_size, 0)
            cols_now = lax.dynamic_slice_in_dim(stripe_cols, first_slot, group_size, 0)
            in_use = (first_slot + jnp.arange(group_size, dtype=jnp.int32) < live_count).astype(
                current.dtype
            )
            values_now = values_now * in_use[:, None, None]
            forward = jnp.einsum("sab,sbn->san", values_now, col_side[cols_now], precision=HIGH)
            backward = jnp.einsum("sba,sbn->san", values_now, row_side[rows_now], precision=HIGH)
            return (row_part.at[rows_now].add(forward), col_part.at[cols_now].add(backward))

        start_parts = (
            jnp.zeros((row_count * owned_blocks, BS, block_width), current.dtype),
            jnp.zeros((col_length, BS, block_width), current.dtype),
        )
        row_part, col_part = lax.fori_loop(0, group_total, group_step, start_parts)
        row_sum = lax.psum_scatter(row_part, "row", scatter_dimension=0, tiled=True)
        col_sum = lax.psum_scatter(col_part, "col", scatter_dimension=0, tiled=True)
        image_block = degree[:, None] * current - (row_sum + col_sum).reshape(
            local_rows, block_width
        )
        stacked = jnp.concatenate(basis_list, axis=1)
        alpha_block = lax.psum(local_gram(current, image_block), ("row", "col")) / total_rows
        image_block = image_block - jnp.dot(current, alpha_block, precision=HIGH)
        if iteration > 0:
            image_block = image_block - jnp.dot(basis_list[-2], beta_list[-1].T, precision=HIGH)
        projection = lax.psum(local_gram(stacked, image_block), ("row", "col")) / total_rows
        image_block = image_block - jnp.dot(stacked, projection, precision=HIGH)
        norm_gram = lax.psum(local_gram(image_block, image_block), ("row", "col")) / total_rows
        lower_factor = jnp.linalg.cholesky(norm_gram)
        current = lax.linalg.triangular_solve(
            lower_factor, image_block, left_side=False, lower=True, transpose_a=True
        )
        alpha_list.append(alpha_block)
        beta_list.append(lower_factor.T)
        basis_list.append(current)
    return (jnp.stack(alpha_list), jnp.stack(beta_list), current)


def solution(mesh):
    return jax.shard_map(
        on_device,
        mesh=mesh,
        in_specs=(
            P(("row", "col"), None),
            P(("row", "col")),
            P(("row", "col"), None),
            P(("row", "col")),
            P(("row", "col")),
            P(("row", "col"), None),
            P(("row", "col")),
        ),
        out_specs=(P(), P(), P(("row", "col"), None)),
        check_vma=False,
    )
```

profile of v0, /device:TPU:1, one launch (start us, length us, event | category | flops | bytes accessed | tf_op | source)
XLA Modules:
  0.0 1838.1 jit_solution(1668707022313247895)
XLA Ops:
  9.2 145.2 %all-reduce.8.cloned.1.call-done = f32[128,128]{0,1:T(8,128)} async-done(((f32[128,128]{0,1:T(8,128)}), f32[128,128]{0,1:T(8,128)}) %all-reduce.8.cloned.1.call-update) | async-done | bytes 65552 | tf_op jit(solution)/shard_map/psum | solution.py:27
  156.2 11.7 cholesky.59
  169.2 9.8 custom-call.7
  181.6 6.6 copy.70
  189.9 20.1 %fusion.27 = s32[384]{0:T(512)S(1)} fusion(s32[384]{0:T(512)S(1)} %copy-done.16, s32[]{:T(128)} %bitcast.7, s32[]{:T(128)} %bitcast.8, s32[]{:T(128)} %bitcast.9, s32[]{:T(128)} %bitcast.10, s32[]{:T(128)} %bitcast.11, s32[]{:T(128)} %bitcast.12, s32[]{:T(128)} %bitcast.13, s32[]{:T(128)} %bitcast.14, s32[]{:T(128)} %bitcast.15, s32[]{:T(128)} %bitcast.16, ...), kind=kLoop, calls=%fused_computation.85 | loop fusion | flops 31104 | bytes 3200 | tf_op jit(solution)/shard_map/add | solution.py:26
  210.0 37.6 %all-gather.5.cloned.1.call-done = f32[64,64,128]{2,1,0:T(8,128)} async-done(((f32[4,64,128]{2,1,0:T(8,128)}), f32[64,64,128]{2,1,0:T(8,128)}) %all-gather.5.cloned.1.call-update) | async-done | bytes 2097168 | tf_op jit(solution)/shard_map/all_gather | solution.py:38
  249.3 130.8 %while.24 = (s32[]{:T(128)}, f32[32,64,128]{2,1,0:T(8,128)S(1)}, f32[64,64,128]{2,1,0:T(8,128)}, s32[]{:T(128)}, s32[384]{0:T(512)S(1)}, /*index=5*/f32[384,4096...) while((s32[]{:T(128)}, f32[32,64,128]{2,1,0:T(8,128)S(1)}, ...), condition=%wide.region_6.9_spmd, body=%wide.region_3.0_spmd.sunk | while | flops 1613237376 | bytes 96483616 | solution.py:62
  252.2 4.6 copy.103
  256.8 4.5 gather_fusion
  261.2 12.2 fusion.90
  273.4 13.5 scatter_fusion
  289.7 10.0 fusion.91
  299.8 13.5 scatter_fusion.1
  317.3 4.6 copy.103
  321.9 4.5 gather_fusion
  326.4 12.2 fusion.90
  338.5 13.5 scatter_fusion
  354.9 10.0 fusion.91
  364.9 13.5 scatter_fusion.1
  381.8 94.0 %reduce-scatter.5.cloned.1.call-done = f32[4,64,128]{2,1,0:T(8,128)} async-done(((f32[32,64,128]{2,1,0:T(8,128)}), f32[4,64,128]{2,1,0:T(8,128)}) %reduce-scatter.5.cloned.1.call-update) | async-done | bytes 131088 | tf_op jit(solution)/shard_map/reduce_scatter | solution.py:63
  475.7 77.8 %reduce-scatter.7.cloned.1.call-done = f32[4,64,128]{2,1,0:T(8,128)} async-done(((f32[64,64,128]{2,1,0:T(8,128)}), f32[4,64,128]{2,1,0:T(8,128)}) %reduce-scatter.7.cloned.1.call-update) | async-done | bytes 131088 | tf_op jit(solution)/shard_map/reduce_scatter | solution.py:64
  555.6 141.9 %all-reduce.10.cloned.1.call-done = f32[128,128]{0,1:T(8,128)} async-done(((f32[128,128]{0,1:T(8,128)}), f32[128,128]{0,1:T(8,128)}) %all-reduce.10.cloned.1.call-update) | async-done | bytes 65552 | tf_op jit(solution)/shard_map/psum | solution.py:69
  699.6 138.6 %all-reduce.12.cloned.1.call-done = f32[128,128]{0,1:T(8,128)} async-done(((f32[128,128]{0,1:T(8,128)}), f32[128,128]{0,1:T(8,128)}) %all-reduce.12.cloned.1.call-update) | async-done | bytes 65552 | tf_op jit(solution)/shard_map/psum | solution.py:73
  840.4 137.9 %all-reduce.14.cloned.1.call-done = f32[128,128]{0,1:T(8,128)} async-done(((f32[128,128]{0,1:T(8,128)}), f32[128,128]{0,1:T(8,128)}) %all-reduce.14.cloned.1.call-update) | async-done | bytes 65552 | tf_op jit(solution)/shard_map/psum | solution.py:75
  980.0 11.7 cholesky.70
  993.6 9.8 custom-call.8
  1005.1 20.4 %all-gather.11.cloned.1.call-done = f32[32,64,128]{2,1,0:T(8,128)} async-done(((f32[4,64,128]{2,1,0:T(8,128)}), f32[32,64,128]{2,1,0:T(8,128)}) %all-gather.11.cloned.1.call-update) | async-done | bytes 1048592 | tf_op jit(solution)/shard_map/all_gather | solution.py:37
  1025.5 46.2 %all-gather.9.cloned.1.call-done = f32[64,64,128]{2,1,0:T(8,128)} async-done(((f32[4,64,128]{2,1,0:T(8,128)}), f32[64,64,128]{2,1,0:T(8,128)}) %all-gather.9.cloned.1.call-update) | async-done | bytes 2097168 | tf_op jit(solution)/shard_map/all_gather | solution.py:38
  1073.5 130.6 %while.25 = (s32[]{:T(128)}, f32[32,64,128]{2,1,0:T(8,128)S(1)}, f32[64,64,128]{2,1,0:T(8,128)}, s32[]{:T(128)}, s32[384]{0:T(512)S(1)}, /*index=5*/f32[384,4096...) while((s32[]{:T(128)}, f32[32,64,128]{2,1,0:T(8,128)S(1)}, ...), condition=%wide.region_15.18_spmd, body=%wide.region_12.0_spmd.sunk | while | flops 1613237376 | bytes 96483616 | solution.py:62
  1076.4 4.6 copy.104
  1080.9 4.5 gather_fusion.2
  1085.4 12.2 fusion.96
  1097.6 13.5 scatter_fusion.2
  1113.9 10.0 fusion.97
  1123.9 13.5 scatter_fusion.3
  1141.5 4.6 copy.104
  1146.1 4.5 gather_fusion.2
  1150.5 12.2 fusion.96
  1162.7 13.5 scatter_fusion.2
  1179.0 10.0 fusion.97
  1189.1 13.5 scatter_fusion.3
  1205.7 94.0 %reduce-scatter.9.cloned.1.call-done = f32[4,64,128]{2,1,0:T(8,128)} async-done(((f32[32,64,128]{2,1,0:T(8,128)}), f32[4,64,128]{2,1,0:T(8,128)}) %reduce-scatter.9.cloned.1.call-update) | async-done | bytes 131088 | tf_op jit(solution)/shard_map/reduce_scatter | solution.py:63
  1299.7 77.7 %reduce-scatter.11.cloned.1.call-done = f32[4,64,128]{2,1,0:T(8,128)} async-done(((f32[64,64,128]{2,1,0:T(8,128)}), f32[4,64,128]{2,1,0:T(8,128)}) %reduce-scatter.11.cloned.1.call-update) | async-done | bytes 131088 | tf_op jit(solution)/shard_map/reduce_scatter | solution.py:64
  1379.5 142.1 %all-reduce.16.cloned.1.call-done = f32[128,128]{0,1:T(8,128)} async-done(((f32[128,128]{0,1:T(8,128)}), f32[128,128]{0,1:T(8,128)}) %all-reduce.16.cloned.1.call-update) | async-done | bytes 65552 | tf_op jit(solution)/shard_map/psum | solution.py:69
  1525.6 138.9 %all-reduce.18.cloned.1.call-done = f32[256,128]{1,0:T(8,128)} async-done(((f32[256,128]{1,0:T(8,128)}), f32[256,128]{1,0:T(8,128)}) %all-reduce.18.cloned.1.call-update) | async-done | bytes 131088 | tf_op jit(solution)/shard_map/psum | solution.py:73
  1667.5 137.4 %all-reduce.20.cloned.1.call-done = f32[128,128]{0,1:T(8,128)} async-done(((f32[128,128]{0,1:T(8,128)}), f32[128,128]{0,1:T(8,128)}) %all-reduce.20.cloned.1.call-update) | async-done | bytes 65552 | tf_op jit(solution)/shard_map/psum | solution.py:75
  1806.6 11.7 cholesky.81
  1820.5 9.8 custom-call.9
  (161 shorter events, 68.0 us)
Async XLA Ops:
  7.2 0.9 copy-start
  7.2 147.2 %all-reduce.8.cloned.1.call-start = ((), (), s32[]{:S(2)}) async-start(), calls=%async_computation.4 | async-start | bytes 131072 | tf_op jit(solution)/shard_map/psum | solution.py:27
  9.1 200.9 %all-gather.7.cloned.1.call-start = ((), (), s32[]{:S(2)}) async-start(), calls=%async_computation.6 | async-start | bytes 1179648 | tf_op jit(solution)/shard_map/all_gather | solution.py:37
  180.2 67.4 %all-gather.5.cloned.1.call-start = ((), (), s32[]{:S(2)}) async-start(), calls=%async_computation.5 | async-start | bytes 2228224 | tf_op jit(solution)/shard_map/all_gather | solution.py:38
  180.9 294.9 %reduce-scatter.5.cloned.1.call-start = ((), (), s32[]{:S(2)}) async-start(), calls=%async_computation.7 | async-start | bytes 1179648 | tf_op jit(solution)/shard_map/reduce_scatter | solution.py:63
  181.6 6.6 copy-start.17
  181.6 8.3 copy-start.16
  181.6 67.6 %copy-start.15 = (s32[384]{0:T(512)S(1)}, s32[384]{0:T(512)}, u32[]{:S(2)}) copy-start(s32[384]{0:T(512)} %param.17) | copy-start | bytes 4612
  249.3 305.3 %copy-start.14 = (f32[256]{0:T(256)S(1)}, f32[256]{0:T(256)}, u32[]{:S(2)}) copy-start(f32[256]{0:T(256)} %param.15) | copy-start | bytes 3076
  273.4 13.5 copy-start.4
  289.7 10.0 copy-start.8
  313.3 1.3 copy-start.9
  338.5 13.5 copy-start.4
  354.9 10.0 copy-start.8
  378.4 1.3 copy-start.9
  380.1 1.0 copy-start.3
  381.1 172.4 %reduce-scatter.7.cloned.1.call-start = ((), (), s32[]{:S(2)}) async-start(), calls=%async_computation.8 | async-start | bytes 2228224 | tf_op jit(solution)/shard_map/reduce_scatter | solution.py:64
  381.7 315.8 %all-reduce.10.cloned.1.call-start = ((), (), s32[]{:S(2)}) async-start(), calls=%async_computation.9 | async-start | bytes 131072 | tf_op jit(solution)/shard_map/psum | solution.py:69
  555.6 282.7 %all-reduce.12.cloned.1.call-start = ((), (), s32[]{:S(2)}) async-start(), calls=%async_computation.10 | async-start | bytes 131072 | tf_op jit(solution)/shard_map/psum | solution.py:73
  699.6 278.7 %all-reduce.14.cloned.1.call-start = ((), (), s32[]{:S(2)}) async-start(), calls=%async_computation.11 | async-start | bytes 131072 | tf_op jit(solution)/shard_map/psum | solution.py:75
  840.3 185.2 %all-gather.11.cloned.1.call-start = ((), (), s32[]{:S(2)}) async-start(), calls=%async_computation.13 | async-start | bytes 1179648 | tf_op jit(solution)/shard_map/all_gather | solution.py:37
  991.8 33.8 %copy-start.10 = (f32[128,128]{1,0:T(8,128)}, f32[128,128]{1,0:T(8,128)S(1)}, u32[]{:S(2)}) copy-start(f32[128,128]{1,0:T(8,128)S(1)} %cholesky.70) | copy-start | bytes 196612
  1004.5 67.3 %all-gather.9.cloned.1.call-start = ((), (), s32[]{:S(2)}) async-start(), calls=%async_computation.12 | async-start | bytes 2228224 | tf_op jit(solution)/shard_map/all_gather | solution.py:38
  1005.1 294.6 %reduce-scatter.9.cloned.1.call-start = ((), (), s32[]{:S(2)}) async-start(), calls=%async_computation.14 | async-start | bytes 1179648 | tf_op jit(solution)/shard_map/reduce_scatter | solution.py:63
  1097.6 13.5 copy-start.5
  1113.9 10.0 copy-start.6
  1137.5 1.3 copy-start.7
  1162.7 13.5 copy-start.5
  1179.0 10.0 copy-start.6
  1202.6 1.3 copy-start.7
  1204.1 1.0 copy-start.2
  1204.1 175.4 %copy-start.12 = (f32[128,128]{0,1:T(8,128)S(1)}, f32[128,128]{0,1:T(8,128)}, u32[]{:S(2)}) copy-start(f32[128,128]{0,1:T(8,128)} %all-reduce.10.cloned.1.call-done) | copy-start | bytes 196612
  1204.1 318.6 %copy-start.11 = (f32[128,128]{1,0:T(8,128)S(1)}, f32[128,128]{1,0:T(8,128)}, u32[]{:S(2)}) copy-start(f32[128,128]{1,0:T(8,128)} %copy-done.10) | copy-start | bytes 196612
  1204.1 615.6 %copy-start.13 = (f32[1,128,128]{1,2,0:T(8,128)S(1)}, f32[1,128,128]{1,2,0:T(8,128)}, u32[]{:S(2)}) copy-start(f32[1,128,128]{1,2,0:T(8,128)} %get-tuple-element.212) | copy-start | bytes 196612
  1205.1 172.3 %reduce-scatter.11.cloned.1.call-start = ((), (), s32[]{:S(2)}) async-start(), calls=%async_computation.15 | async-start | bytes 2228224 | tf_op jit(solution)/shard_map/reduce_scatter | solution.py:64
  1205.1 626.2 %copy-start.1 = (f32[256,128]{1,0:T(8,128)S(1)}, f32[256,128]{1,0:T(8,128)}, u32[]{:S(2)}) copy-start(f32[256,128]{1,0:T(8,128)} %param.14) | copy-start | bytes 393220
  1205.7 315.9 %all-reduce.16.cloned.1.call-start = ((), (), s32[]{:S(2)}) async-start(), calls=%async_computation.16 | async-start | bytes 131072 | tf_op jit(solution)/shard_map/psum | solution.py:69
  1379.5 285.0 %all-reduce.18.cloned.1.call-start = ((), (), s32[]{:S(2)}) async-start(), calls=%async_computation.17 | async-start | bytes 262144 | tf_op jit(solution)/shard_map/psum | solution.py:73
  1524.7 280.2 %all-reduce.20.cloned.1.call-start = ((), (), s32[]{:S(2)}) async-start(), calls=%async_computation.18 | async-start | bytes 131072 | tf_op jit(solution)/shard_map/psum | solution.py:75
Sparse Core Ops, SparseCore 0:
  13.3 141.0 all-reduce.7
  180.3 20.8 all-gather.6
  204.1 43.3 all-gather.4
  381.2 94.4 reduce-scatter.4
  479.2 74.2 reduce-scatter.6
  558.7 138.7 all-reduce.9
  703.6 134.6 all-reduce.11
  843.6 134.6 all-reduce.13
  1004.6 20.8 all-gather.10
  1028.3 43.4 all-gather.8
  1205.2 94.4 reduce-scatter.8
  1303.2 74.2 reduce-scatter.10
  1382.8 138.7 all-reduce.15
  1527.5 136.8 all-reduce.17
  1669.6 135.2 all-reduce.19
where the time goes:
time: 1850 us; the launch traced here: 1840 us
  waiting for transfers between devices  1430 us (77%)
  other arithmetic  209 us (11%)
  matrix products  102 us (6%)
  local copies, waits for them, and re-layouts  78.1 us (4%)
    psum x2, waiting for transfers between devices, on_device(): lax.psum(local_gram(current, image_block), ('row', 'col')) / total_rows  284 us
    psum x2, waiting for transfers between devices, on_device(): lax.psum(local_gram(stacked, image_block), ('row', 'col')) / total_rows  278 us
    psum x2, waiting for transfers between devices, on_device(): lax.psum(local_gram(image_block, image_block), ('row', 'col')) / total_rows  275 us
    reduce_scatter x2, waiting for transfers between devices, on_device(): row_sum = lax.psum_scatter(row_part, 'row', scatter_dimension=0, tiled=True)  188 us
    reduce_scatter x2, waiting for transfers between devices, on_device(): col_sum = lax.psum_scatter(col_part, 'col', scatter_dimension=0, tiled=True)  155 us
    psum x1, waiting for transfers between devices, on_device(): lax.psum(local_gram(start_block, start_block), ('row', 'col')) / total_rows  145 us
    all_gather x2, waiting for transfers between devices, on_device(): col_side = lax.all_gather(owned_rows, 'col', axis=0, tiled=True)  83.8 us
    scatter-add x4, other arithmetic, group_step(): col_part.at[cols_now].add(backward)  54 us
  transfers between devices with their start and end apart: 15, of which 14 were waited for; matrix products, arithmetic and copies ran while one was open for 2% of the time, Pallas kernels for 0%

commit v1 on v0

--- a/solution.py
+++ b/solution.py
@@ -24,7 +24,8 @@
     live_count = live_blocks[0]
     flat_need = need_lists.reshape(-1)
     stripe_cols = block_slots // list_length * owned_blocks + flat_need[block_slots]
-    start_gram = lax.psum(local_gram(start_block, start_block), ("row", "col")) / total_rows
+    expand_tails = lambda slab_in: jnp.sum(jax.lax.all_gather(slab_in, ("row", "col")), 0)
+    start_gram = expand_tails(local_gram(start_block, start_block)) / total_rows
     lower_factor = jnp.linalg.cholesky(start_gram)
     current = lax.linalg.triangular_solve(
         lower_factor, start_block, left_side=False, lower=True, transpose_a=True

time: 1850 us -> 1780 us (0.962)
  waiting for transfers between devices: 1430 us -> 1360 us
    psum x1 -> x0, waiting for transfers between devices: 145 us -> none  [on_device(): lax.psum(local_gram(start_block, start_block), ('row', 'col')) / total_rows]
    all_gather x0 -> x1, waiting for transfers between devices: none -> 76.4 us  [on_device(): jax.lax.all_gather(slab_in, ('row', 'col'))]
where the time goes in v1:
time: 1780 us; the launch traced here: 1770 us
  waiting for transfers between devices  1360 us (76%)
  other arithmetic  211 us (12%)
  matrix products  102 us (6%)
  local copies, waits for them, and re-layouts  78.2 us (4%)
    psum x2, waiting for transfers between devices, on_device(): lax.psum(local_gram(current, image_block), ('row', 'col')) / total_rows  286 us
    psum x2, waiting for transfers between devices, on_device(): lax.psum(local_gram(image_block, image_block), ('row', 'col')) / total_rows  277 us
    psum x2, waiting for transfers between devices, on_device(): lax.psum(local_gram(stacked, image_block), ('row', 'col')) / total_rows  276 us
    reduce_scatter x2, waiting for transfers between devices, on_device(): row_sum = lax.psum_scatter(row_part, 'row', scatter_dimension=0, tiled=True)  188 us
    reduce_scatter x2, waiting for transfers between devices, on_device(): col_sum = lax.psum_scatter(col_part, 'col', scatter_dimension=0, tiled=True)  155 us
    all_gather x2, waiting for transfers between devices, on_device(): col_side = lax.all_gather(owned_rows, 'col', axis=0, tiled=True)  83.6 us
    all_gather x1, waiting for transfers between devices, on_device(): jax.lax.all_gather(slab_in, ('row', 'col'))  76.4 us
    scatter-add x4, other arithmetic, group_step(): col_part.at[cols_now].add(backward)  54 us
  transfers between devices with their start and end apart: 15, of which 14 were waited for; matrix products, arithmetic and copies ran while one was open for 2% of the time, Pallas kernels for 0%

profile of v1, /device:TPU:1, one launch (start us, length us, event | category | flops | bytes accessed | tf_op | source)
XLA Modules:
  0.0 1772.2 jit_solution(3497929272974036130)
XLA Ops:
  9.2 76.4 %all-gather.15.cloned.1.call-done = f32[16384,128]{1,0:T(8,128)} async-done(((f32[128,128]{1,0:T(8,128)}), f32[16384,128]{1,0:T(8,128)}) %all-gather.15.cloned.1.call-update) | async-done | bytes 8388624 | tf_op jit(solution)/shard_map/all_gather | solution.py:27
  89.6 11.7 cholesky.59
  102.6 9.8 custom-call.7
  115.0 6.6 copy.68
  123.3 20.1 %fusion.27 = s32[384]{0:T(512)S(1)} fusion(s32[384]{0:T(512)S(1)} %copy-done.16, s32[]{:T(128)} %bitcast.8, s32[]{:T(128)} %bitcast.9, s32[]{:T(128)} %bitcast.10, s32[]{:T(128)} %bitcast.11, s32[]{:T(128)} %bitcast.12, s32[]{:T(128)} %bitcast.13, s32[]{:T(128)} %bitcast.14, s32[]{:T(128)} %bitcast.15, s32[]{:T(128)} %bitcast.16, s32[]{:T(128)} %bitcast.17, ...), kind=kLoop, calls=%fused_computation.85 | loop fusion | flops 31104 | bytes 3200 | tf_op jit(solution)/shard_map/add | solution.py:26
  143.4 37.6 %all-gather.7.cloned.1.call-done = f32[64,64,128]{2,1,0:T(8,128)} async-done(((f32[4,64,128]{2,1,0:T(8,128)}), f32[64,64,128]{2,1,0:T(8,128)}) %all-gather.7.cloned.1.call-update) | async-done | bytes 2097168 | tf_op jit(solution)/shard_map/all_gather | solution.py:39
  182.6 130.8 %while.24 = (s32[]{:T(128)}, f32[32,64,128]{2,1,0:T(8,128)S(1)}, f32[64,64,128]{2,1,0:T(8,128)}, s32[]{:T(128)}, s32[384]{0:T(512)S(1)}, /*index=5*/f32[384,4096...) while((s32[]{:T(128)}, f32[32,64,128]{2,1,0:T(8,128)S(1)}, ...), condition=%wide.region_6.9_spmd, body=%wide.region_3.0_spmd.sunk | while | flops 1613237376 | bytes 96483616 | solution.py:63
  185.6 4.6 copy.100
  190.1 4.5 gather_fusion
  194.6 12.2 fusion.90
  206.8 13.5 scatter_fusion
  223.1 10.0 fusion.91
  233.1 13.5 scatter_fusion.1
  250.7 4.6 copy.100
  255.3 4.5 gather_fusion
  259.7 12.2 fusion.90
  271.9 13.5 scatter_fusion
  288.2 10.0 fusion.91
  298.3 13.5 scatter_fusion.1
  315.1 94.0 %reduce-scatter.5.cloned.1.call-done = f32[4,64,128]{2,1,0:T(8,128)} async-done(((f32[32,64,128]{2,1,0:T(8,128)}), f32[4,64,128]{2,1,0:T(8,128)}) %reduce-scatter.5.cloned.1.call-update) | async-done | bytes 131088 | tf_op jit(solution)/shard_map/reduce_scatter | solution.py:64
  409.1 77.5 %reduce-scatter.7.cloned.1.call-done = f32[4,64,128]{2,1,0:T(8,128)} async-done(((f32[64,64,128]{2,1,0:T(8,128)}), f32[4,64,128]{2,1,0:T(8,128)}) %reduce-scatter.7.cloned.1.call-update) | async-done | bytes 131088 | tf_op jit(solution)/shard_map/reduce_scatter | solution.py:65
  488.6 142.7 %all-reduce.7.cloned.1.call-done = f32[128,128]{0,1:T(8,128)} async-done(((f32[128,128]{0,1:T(8,128)}), f32[128,128]{0,1:T(8,128)}) %all-reduce.7.cloned.1.call-update) | async-done | bytes 65552 | tf_op jit(solution)/shard_map/psum | solution.py:70
  633.4 137.9 %all-reduce.9.cloned.1.call-done = f32[128,128]{0,1:T(8,128)} async-done(((f32[128,128]{0,1:T(8,128)}), f32[128,128]{0,1:T(8,128)}) %all-reduce.9.cloned.1.call-update) | async-done | bytes 65552 | tf_op jit(solution)/shard_map/psum | solution.py:74
  773.4 138.6 %all-reduce.11.cloned.1.call-done = f32[128,128]{0,1:T(8,128)} async-done(((f32[128,128]{0,1:T(8,128)}), f32[128,128]{0,1:T(8,128)}) %all-reduce.11.cloned.1.call-update) | async-done | bytes 65552 | tf_op jit(solution)/shard_map/psum | solution.py:76
  913.8 11.7 cholesky.70
  927.4 9.8 custom-call.8
  938.9 20.4 %all-gather.13.cloned.1.call-done = f32[32,64,128]{2,1,0:T(8,128)} async-done(((f32[4,64,128]{2,1,0:T(8,128)}), f32[32,64,128]{2,1,0:T(8,128)}) %all-gather.13.cloned.1.call-update) | async-done | bytes 1048592 | tf_op jit(solution)/shard_map/all_gather | solution.py:38
  959.3 46.0 %all-gather.11.cloned.1.call-done = f32[64,64,128]{2,1,0:T(8,128)} async-done(((f32[4,64,128]{2,1,0:T(8,128)}), f32[64,64,128]{2,1,0:T(8,128)}) %all-gather.11.cloned.1.call-update) | async-done | bytes 2097168 | tf_op jit(solution)/shard_map/all_gather | solution.py:39
  1007.0 130.6 %while.25 = (s32[]{:T(128)}, f32[32,64,128]{2,1,0:T(8,128)S(1)}, f32[64,64,128]{2,1,0:T(8,128)}, s32[]{:T(128)}, s32[384]{0:T(512)S(1)}, /*index=5*/f32[384,4096...) while((s32[]{:T(128)}, f32[32,64,128]{2,1,0:T(8,128)S(1)}, ...), condition=%wide.region_15.18_spmd, body=%wide.region_12.0_spmd.sunk | while | flops 1613237376 | bytes 96483616 | solution.py:63
  1009.9 4.6 copy.101
  1014.5 4.5 gather_fusion.2
  1019.0 12.2 fusion.96
  1031.1 13.5 scatter_fusion.2
  1047.5 10.0 fusion.97
  1057.5 13.5 scatter_fusion.3
  1075.1 4.6 copy.101
  1079.7 4.5 gather_fusion.2
  1084.1 12.2 fusion.96
  1096.3 13.5 scatter_fusion.2
  1112.6 10.0 fusion.97
  1122.7 13.5 scatter_fusion.3
  1139.3 94.0 %reduce-scatter.9.cloned.1.call-done = f32[4,64,128]{2,1,0:T(8,128)} async-done(((f32[32,64,128]{2,1,0:T(8,128)}), f32[4,64,128]{2,1,0:T(8,128)}) %reduce-scatter.9.cloned.1.call-update) | async-done | bytes 131088 | tf_op jit(solution)/shard_map/reduce_scatter | solution.py:64
  1233.3 77.5 %reduce-scatter.11.cloned.1.call-done = f32[4,64,128]{2,1,0:T(8,128)} async-done(((f32[64,64,128]{2,1,0:T(8,128)}), f32[4,64,128]{2,1,0:T(8,128)}) %reduce-scatter.11.cloned.1.call-update) | async-done | bytes 131088 | tf_op jit(solution)/shard_map/reduce_scatter | solution.py:65
  1312.8 142.8 %all-reduce.13.cloned.1.call-done = f32[128,128]{0,1:T(8,128)} async-done(((f32[128,128]{0,1:T(8,128)}), f32[128,128]{0,1:T(8,128)}) %all-reduce.13.cloned.1.call-update) | async-done | bytes 65552 | tf_op jit(solution)/shard_map/psum | solution.py:70
  1459.6 138.2 %all-reduce.15.cloned.1.call-done = f32[256,128]{1,0:T(8,128)} async-done(((f32[256,128]{1,0:T(8,128)}), f32[256,128]{1,0:T(8,128)}) %all-reduce.15.cloned.1.call-update) | async-done | bytes 131088 | tf_op jit(solution)/shard_map/psum | solution.py:74
  1600.8 138.1 %all-reduce.17.cloned.1.call-done = f32[128,128]{0,1:T(8,128)} async-done(((f32[128,128]{0,1:T(8,128)}), f32[128,128]{0,1:T(8,128)}) %all-reduce.17.cloned.1.call-update) | async-done | bytes 65552 | tf_op jit(solution)/shard_map/psum | solution.py:76
  1740.7 11.7 cholesky.81
  1754.6 9.8 custom-call.9
  (163 shorter events, 70.2 us)
Async XLA Ops:
  7.2 0.9 copy-start
  7.2 78.4 %all-gather.15.cloned.1.call-start = ((), (), s32[]{:S(2)}) async-start(), calls=%async_computation.18 | async-start | bytes 8454144 | tf_op jit(solution)/shard_map/all_gather | solution.py:27
  9.1 134.2 %all-gather.9.cloned.1.call-start = ((), (), s32[]{:S(2)}) async-start(), calls=%async_computation.5 | async-start | bytes 1179648 | tf_op jit(solution)/shard_map/all_gather | solution.py:38
  113.5 67.4 %all-gather.7.cloned.1.call-start = ((), (), s32[]{:S(2)}) async-start(), calls=%async_computation.4 | async-start | bytes 2228224 | tf_op jit(solution)/shard_map/all_gather | solution.py:39
  114.3 294.8 %reduce-scatter.5.cloned.1.call-start = ((), (), s32[]{:S(2)}) async-start(), calls=%async_computation.6 | async-start | bytes 1179648 | tf_op jit(solution)/shard_map/reduce_scatter | solution.py:64
  115.0 6.6 copy-start.17
  115.0 8.3 copy-start.16
  115.0 67.6 %copy-start.15 = (s32[384]{0:T(512)S(1)}, s32[384]{0:T(512)}, u32[]{:S(2)}) copy-start(s32[384]{0:T(512)} %param.17) | copy-start | bytes 4612
  182.6 305.0 %copy-start.14 = (f32[256]{0:T(256)S(1)}, f32[256]{0:T(256)}, u32[]{:S(2)}) copy-start(f32[256]{0:T(256)} %param.15) | copy-start | bytes 3076
  206.8 13.5 copy-start.4
  223.1 10.0 copy-start.8
  246.6 1.3 copy-start.9
  271.9 13.5 copy-start.4
  288.2 10.0 copy-start.8
  311.8 1.3 copy-start.9
  313.5 1.0 copy-start.3
  314.5 172.1 %reduce-scatter.7.cloned.1.call-start = ((), (), s32[]{:S(2)}) async-start(), calls=%async_computation.7 | async-start | bytes 2228224 | tf_op jit(solution)/shard_map/reduce_scatter | solution.py:65
  315.1 316.2 %all-reduce.7.cloned.1.call-start = ((), (), s32[]{:S(2)}) async-start(), calls=%async_computation.8 | async-start | bytes 131072 | tf_op jit(solution)/shard_map/psum | solution.py:70
  488.6 282.7 %all-reduce.9.cloned.1.call-start = ((), (), s32[]{:S(2)}) async-start(), calls=%async_computation.9 | async-start | bytes 131072 | tf_op jit(solution)/shard_map/psum | solution.py:74
  633.4 278.7 %all-reduce.11.cloned.1.call-start = ((), (), s32[]{:S(2)}) async-start(), calls=%async_computation.10 | async-start | bytes 131072 | tf_op jit(solution)/shard_map/psum | solution.py:76
  773.4 186.0 %all-gather.13.cloned.1.call-start = ((), (), s32[]{:S(2)}) async-start(), calls=%async_computation.12 | async-start | bytes 1179648 | tf_op jit(solution)/shard_map/all_gather | solution.py:38
  925.6 33.8 %copy-start.10 = (f32[128,128]{1,0:T(8,128)}, f32[128,128]{1,0:T(8,128)S(1)}, u32[]{:S(2)}) copy-start(f32[128,128]{1,0:T(8,128)S(1)} %cholesky.70) | copy-start | bytes 196612
  938.3 67.0 %all-gather.11.cloned.1.call-start = ((), (), s32[]{:S(2)}) async-start(), calls=%async_computation.11 | async-start | bytes 2228224 | tf_op jit(solution)/shard_map/all_gather | solution.py:39
  938.9 294.4 %reduce-scatter.9.cloned.1.call-start = ((), (), s32[]{:S(2)}) async-start(), calls=%async_computation.13 | async-start | bytes 1179648 | tf_op jit(solution)/shard_map/reduce_scatter | solution.py:64
  1031.1 13.5 copy-start.5
  1047.5 10.0 copy-start.6
  1071.0 1.3 copy-start.7
  1096.3 13.5 copy-start.5
  1112.6 10.0 copy-start.6
  1136.2 1.3 copy-start.7
  1137.7 1.0 copy-start.2
  1137.7 175.1 %copy-start.12 = (f32[128,128]{0,1:T(8,128)S(1)}, f32[128,128]{0,1:T(8,128)}, u32[]{:S(2)}) copy-start(f32[128,128]{0,1:T(8,128)} %all-reduce.7.cloned.1.call-done) | copy-start | bytes 196612
  1137.7 319.1 %copy-start.11 = (f32[128,128]{1,0:T(8,128)S(1)}, f32[128,128]{1,0:T(8,128)}, u32[]{:S(2)}) copy-start(f32[128,128]{1,0:T(8,128)} %copy-done.10) | copy-start | bytes 196612
  1137.7 616.1 %copy-start.13 = (f32[1,128,128]{1,2,0:T(8,128)S(1)}, f32[1,128,128]{1,2,0:T(8,128)}, u32[]{:S(2)}) copy-start(f32[1,128,128]{1,2,0:T(8,128)} %get-tuple-element.212) | copy-start | bytes 196612
  1138.7 172.1 %reduce-scatter.11.cloned.1.call-start = ((), (), s32[]{:S(2)}) async-start(), calls=%async_computation.14 | async-start | bytes 2228224 | tf_op jit(solution)/shard_map/reduce_scatter | solution.py:65
  1138.7 626.7 %copy-start.1 = (f32[256,128]{1,0:T(8,128)S(1)}, f32[256,128]{1,0:T(8,128)}, u32[]{:S(2)}) copy-start(f32[256,128]{1,0:T(8,128)} %param.14) | copy-start | bytes 393220
  1139.2 316.4 %all-reduce.13.cloned.1.call-start = ((), (), s32[]{:S(2)}) async-start(), calls=%async_computation.15 | async-start | bytes 131072 | tf_op jit(solution)/shard_map/psum | solution.py:70
  1312.8 285.0 %all-reduce.15.cloned.1.call-start = ((), (), s32[]{:S(2)}) async-start(), calls=%async_computation.16 | async-start | bytes 262144 | tf_op jit(solution)/shard_map/psum | solution.py:74
  1458.7 280.2 %all-reduce.17.cloned.1.call-start = ((), (), s32[]{:S(2)}) async-start(), calls=%async_computation.17 | async-start | bytes 131072 | tf_op jit(solution)/shard_map/psum | solution.py:76
Sparse Core Ops, SparseCore 0:
  11.7 73.7 all-gather.14
  113.7 21.0 all-gather.8
  137.5 43.4 all-gather.6
  314.6 94.4 reduce-scatter.4
  412.2 74.3 reduce-scatter.6
  492.4 138.8 all-reduce.6
  636.6 134.6 all-reduce.8
  777.3 134.6 all-reduce.10
  938.4 20.8 all-gather.12
  961.9 43.4 all-gather.10
  1138.8 94.4 reduce-scatter.8
  1236.4 74.3 reduce-scatter.10
  1316.8 138.8 all-reduce.12
  1460.8 136.9 all-reduce.14
  1603.7 135.2 all-reduce.16
